TPU v7x, 32 devices: a whole 2x2x4 slice. The times are simulated.
32 devices in a mesh: expert: 8 (over z, y), batch: 4 (over x, core).
Axes of the slice: x: 2, y: 2, z: 4, core: 2. Of those that a mesh axis runs over, the one named last changes fastest.
Arguments:
- tokens: bfloat16 [8192, 1024], P(('expert', 'batch')), may hold values from -6 to 6
- lengths: int32 [32], P(('expert', 'batch')), may hold values from 64 to 256, as said below
- expert_ids: int32 [8192], P(('expert', 'batch')), may hold values from 0 to 7, as said below
- slots: int32 [8192], P(('expert', 'batch')), may hold values from -1 to 31, as said below
- centroids: bfloat16 [8, 1024], replicated, may hold values from -0.125 to 0.125
- sublayer_norm_gain: bfloat16 [2, 8, 1024], P(None, 'expert'), may hold values from 0.5 to 1.5
- sublayer_norm_bias: bfloat16 [2, 8, 1024], P(None, 'expert'), may hold values from -0.59765625 to 0.59765625
- up_weight: bfloat16 [2, 8, 1024, 4096], P(None, 'expert', None, 'batch'), may hold values from -0.1875 to 0.1875
- up_bias: bfloat16 [2, 8, 4096], P(None, 'expert', 'batch'), may hold values from -0.59765625 to 0.59765625
- down_weight: bfloat16 [2, 8, 4096, 1024], P(None, 'expert', 'batch'), may hold values from -0.09375 to 0.09375
- down_bias: bfloat16 [2, 8, 1024], P(None, 'expert'), may hold values from -0.59765625 to 0.59765625
- cotangent: bfloat16 [8192, 1024], P(('expert', 'batch')), may hold values from -6 to 6
Outputs:
- mixed: bfloat16 [8192, 1024], P(('expert', 'batch'))
- tokens_grad: bfloat16 [8192, 1024], P(('expert', 'batch'))
- centroid_grad: float32 [8, 1024], replicated
- gain_grad: float32 [2, 8, 1024], P(None, 'expert')
- shift_grad: float32 [2, 8, 1024], P(None, 'expert')
- up_weight_grad: float32 [2, 8, 1024, 4096], P(None, 'expert', None, 'batch')
- up_bias_grad: float32 [2, 8, 4096], P(None, 'expert', 'batch')
- down_weight_grad: float32 [2, 8, 4096, 1024], P(None, 'expert', 'batch')
- down_bias_grad: float32 [2, 8, 1024], P(None, 'expert')
- gate_mass: float32 [8], replicated
- load: float32 [8], replicated
Inputs may be any that keep to these rules, and one draw needn't show every extreme that they name: `lengths`: one device's sequence has length 256 and one has 64. `expert_ids`: every expert is named somewhere. -1 exactly at padded positions; a device's live positions of one expert have distinct slots; some expert receives 32 positions from every device.
All inputs are finite; a program needn't handle non-finite values.
Results may differ from a plain program's by a relative error of at most 0.017.
Values may be sent and summed in bfloat16 or wider, within the bound.
A program may use at most 128 MiB of HBM per device.

v0:
```python
import jax
import jax.numpy as jnp
from jax import lax
from jax.sharding import PartitionSpec as P


def gelu_exact(values):
    return jax.nn.gelu(values, approximate=False)


def apply_layer_norm(row_block):
    values = row_block.astype(jnp.float32)
    row_mean = jnp.mean(values, axis=-1, keepdims=True)
    centered = values - row_mean
    row_inverse_scale = lax.rsqrt(jnp.mean(centered * centered, axis=-1, keepdims=True) + 1e-05)
    return (centered * row_inverse_scale, row_inverse_scale)


def per_device(
    tokens,
    lengths,
    expert_ids,
    slots,
    centroids,
    sublayer_norm_gain,
    sublayer_norm_bias,
    up_weight,
    up_bias,
    down_weight,
    down_bias,
    cotangent,
):
    tok_rows, width = tokens.shape
    layers = sublayer_norm_gain.shape[0]
    local_count = up_weight.shape[1]
    expert_count = centroids.shape[0]
    capacity = tok_rows // expert_count
    groups = lax.axis_size("expert")
    batches = lax.axis_size("batch")
    position = jnp.arange(tok_rows, dtype=jnp.int32)
    live = (position < lengths[0]).astype(jnp.float32)[:, None]
    target = jnp.where(slots >= 0, expert_ids * capacity + slots, tok_rows)
    source = jnp.full((tok_rows + 1,), -1, jnp.int32).at[target].set(position)[:tok_rows]
    filled = (source >= 0)[:, None]
    safe_source = jnp.maximum(source, 0)
    safe_target = jnp.minimum(target, tok_rows - 1)

    def pack(values):
        return jnp.where(filled, values[safe_source], jnp.zeros((), values.dtype))

    onehot = (expert_ids[:, None] == jnp.arange(expert_count, dtype=jnp.int32)[None, :]).astype(
        jnp.float32
    )
    logits = jnp.einsum("td,ed->te", tokens, centroids, preferred_element_type=jnp.float32)
    gate = jax.nn.sigmoid(jnp.sum(logits * onehot, axis=1))[:, None]
    used = onehot * live
    usage_gate = jnp.sum(used * gate, axis=0)
    usage_count = jnp.sum(used, axis=0)
    gate_total, count_total = lax.psum((usage_gate, usage_count), ("expert", "batch"))

    def expand_hidden(values, expert_layer_step):
        return values[expert_layer_step].astype(jnp.float32)[None, :, None, :]

    arrived = lax.all_to_all(pack(tokens), "expert", split_axis=0, concat_axis=0, tiled=True)
    current = arrived
    inputs = []
    kept = []
    for expert_layer_step in range(layers):
        gathered = lax.all_gather(current, "batch", axis=0, tiled=True)
        row_layout_grid = gathered.reshape(-1, local_count, capacity, width)
        standardized_input, row_inverse_scale = apply_layer_norm(row_layout_grid)
        normalized_rows = (
            standardized_input * expand_hidden(sublayer_norm_gain, expert_layer_step)
            + expand_hidden(sublayer_norm_bias, expert_layer_step)
        ).astype(jnp.bfloat16)
        pre_rows = jnp.einsum(
            "nlcd,ldf->nlcf",
            normalized_rows,
            up_weight[expert_layer_step],
            preferred_element_type=jnp.float32,
        ) + expand_hidden(up_bias, expert_layer_step)
        hidden_parts = (normalized_rows, pre_rows, gelu_exact(pre_rows).astype(jnp.bfloat16))

        def down_part(start, count, activity=hidden_parts[2], expert_layer_step=expert_layer_step):
            return jnp.einsum(
                "nlcf,lfd->nlcd",
                activity,
                down_weight[expert_layer_step],
                preferred_element_type=jnp.float32,
            )

        mixed_part = lax.psum_scatter(
            down_part(jnp.int32(0), lax.axis_size("batch") * groups).astype(jnp.bfloat16),
            "batch",
            scatter_dimension=0,
            tiled=True,
        ).astype(jnp.float32)
        own_grid = current.reshape(groups, local_count, capacity, width).astype(jnp.float32)
        result = (own_grid + mixed_part + expand_hidden(down_bias, expert_layer_step)).astype(
            jnp.bfloat16
        )
        inputs.append(current)
        kept.append(hidden_parts)
        current = result.reshape(tok_rows, width)
    returned = lax.all_to_all(current, "expert", split_axis=0, concat_axis=0, tiled=True)
    expert_tok = returned[safe_target].astype(jnp.float32)
    mixed = (live * (tokens.astype(jnp.float32) + gate * expert_tok)).astype(jnp.bfloat16)
    upstream = cotangent.astype(jnp.float32) * live
    gate_grad = jnp.sum(upstream * expert_tok, axis=1, keepdims=True)
    logit_grad = (gate_grad * gate * (1.0 - gate)).astype(jnp.bfloat16)
    route_grad = (onehot * logit_grad.astype(jnp.float32)).astype(jnp.bfloat16)
    centroid_part = jnp.einsum("te,td->ed", route_grad, tokens, preferred_element_type=jnp.float32)
    gate_input = jnp.einsum("te,ed->td", route_grad, centroids, preferred_element_type=jnp.float32)
    expert_grad = (gate * upstream).astype(jnp.bfloat16)
    grad_rows = lax.all_to_all(pack(expert_grad), "expert", split_axis=0, concat_axis=0, tiled=True)
    gain_parts = [None] * layers
    shift_parts = [None] * layers
    down_bias_parts = [None] * layers
    up_weight_grads = [None] * layers
    up_bias_grads = [None] * layers
    down_weight_grads = [None] * layers
    for expert_layer_step in range(layers - 1, -1, -1):
        own_rows = inputs[expert_layer_step]
        grads_all = lax.all_gather(grad_rows, "batch", axis=0, tiled=True).reshape(
            -1, local_count, capacity, width
        )
        normed, pre_act, activity = kept[expert_layer_step]
        act_grad = jnp.einsum(
            "nlcd,lfd->nlcf",
            grads_all,
            down_weight[expert_layer_step],
            preferred_element_type=jnp.float32,
        )
        pre_grad = jax.vjp(gelu_exact, pre_act)[1](act_grad)[0].astype(jnp.bfloat16)
        down_weight_grads[expert_layer_step] = jnp.einsum(
            "nlcf,nlcd->lfd", activity, grads_all, preferred_element_type=jnp.float32
        )
        up_weight_grads[expert_layer_step] = jnp.einsum(
            "nlcd,nlcf->ldf", normed, pre_grad, preferred_element_type=jnp.float32
        )
        up_bias_grads[expert_layer_step] = jnp.sum(pre_grad.astype(jnp.float32), axis=(0, 2))

        def up_part(start, count, pre_grad=pre_grad, expert_layer_step=expert_layer_step):
            return jnp.einsum(
                "nlcf,ldf->nlcd",
                pre_grad,
                up_weight[expert_layer_step],
                preferred_element_type=jnp.float32,
            )

        normed_grad = lax.psum_scatter(
            up_part(jnp.int32(0), lax.axis_size("batch") * groups).astype(jnp.bfloat16),
            "batch",
            scatter_dimension=0,
            tiled=True,
        ).astype(jnp.float32)
        out_grad = grad_rows.reshape(groups, local_count, capacity, width).astype(jnp.float32)
        down_bias_parts[expert_layer_step] = jnp.sum(out_grad, axis=(0, 2))
        own_hat, own_scale = apply_layer_norm(
            own_rows.reshape(groups, local_count, capacity, width)
        )
        gain_parts[expert_layer_step] = jnp.sum(normed_grad * own_hat, axis=(0, 2))
        shift_parts[expert_layer_step] = jnp.sum(normed_grad, axis=(0, 2))
        hat_grad = normed_grad * expand_hidden(sublayer_norm_gain, expert_layer_step)
        row_grad = own_scale * (
            hat_grad
            - jnp.mean(hat_grad, axis=-1, keepdims=True)
            - own_hat * jnp.mean(hat_grad * own_hat, axis=-1, keepdims=True)
        )
        grad_rows = (out_grad + row_grad).astype(jnp.bfloat16).reshape(tok_rows, width)
    gain_grad, shift_grad, down_bias_grad = lax.psum(
        (jnp.stack(gain_parts), jnp.stack(shift_parts), jnp.stack(down_bias_parts)), "batch"
    )
    token_back = lax.all_to_all(grad_rows, "expert", split_axis=0, concat_axis=0, tiled=True)
    tokens_grad = (
        upstream + gate_input + live * token_back[safe_target].astype(jnp.float32)
    ).astype(jnp.bfloat16)
    centroid_grad = lax.psum(centroid_part, ("expert", "batch"))
    denominator = jnp.float32(capacity * groups * batches)
    gate_mass = gate_total / denominator
    load = count_total / denominator
    return (
        mixed,
        tokens_grad,
        centroid_grad,
        gain_grad,
        shift_grad,
        jnp.stack(up_weight_grads),
        jnp.stack(up_bias_grads),
        jnp.stack(down_weight_grads),
        down_bias_grad,
        gate_mass,
        load,
    )


def solution(mesh):
    in_specs = (
        P(("expert", "batch"), None),
        P(("expert", "batch")),
        P(("expert", "batch")),
        P(("expert", "batch")),
        P(),
        P(None, "expert", None),
        P(None, "expert", None),
        P(None, "expert", None, "batch"),
        P(None, "expert", "batch"),
        P(None, "expert", "batch", None),
        P(None, "expert", None),
        P(("expert", "batch"), None),
    )
    out_specs = (
        P(("expert", "batch"), None),
        P(("expert", "batch"), None),
        P(),
        P(None, "expert", None),
        P(None, "expert", None),
        P(None, "expert", None, "batch"),
        P(None, "expert", "batch"),
        P(None, "expert", "batch", None),
        P(None, "expert", None),
        P(),
        P(),
    )
    return jax.shard_map(
        per_device, mesh=mesh, in_specs=in_specs, out_specs=out_specs, check_vma=False
    )
```

profile of v0, /device:TPU:0, one launch (start us, length us, event | category | flops | bytes accessed | tf_op | source)
XLA Modules:
  0.0 445.1 jit_solution(8937851070104652665)
XLA Ops:
  7.3 0.7 compare_select_fusion
  8.0 1.4 scatter_custom_fusion
  9.5 2.7 gather_fusion
  12.3 21.7 %all_to_all.42 = bf16[8,32,1024]{2,1,0:T(8,128)(2,1)} all-to-all(bf16[8,32,1024]{2,1,0:T(8,128)(2,1)S(1)} %broadcast_select_fusion.1), channel_id=1, replica_groups=mesh['expert'=8,'batch'=4] {'expert'}, dimensions={0} | all-to-all | bytes 1048576 | tf_op jit(solution)/shard_map/all_to_all | solution.py:64
  34.2 21.6 %all-gather.5.cloned.1.call-done = bf16[1024,1024]{1,0:T(8,128)(2,1)} async-done(((bf16[256,1024]{1,0:T(8,128)(2,1)}), bf16[1024,1024]{1,0:T(8,128)(2,1)}) %all-gather.5.cloned.1.call-update) | async-done | bytes 2097168 | tf_op jit(solution)/shard_map/all_gather | solution.py:69
  55.8 2.1 convert_reduce_fusion.3
  57.9 2.7 multiply_reduce_fusion.1
  60.5 0.8 add_convert_fusion.3
  61.4 2.3 fusion.50
  63.8 2.0 copy-done.44
  65.8 11.8 %convert_bitcast_fusion.3 = bf16[32,1,32,1024]{3,2,0,1:T(8,128)(2,1)} fusion(bf16[2,1,1024,1024]{3,2,1,0:T(8,128)(2,1)S(1)} %copy-done.35, f32[32,32,1024]{2,1,0:T(8,128)S(1)} %fusion.50, f32[1024]{0:T(1024)S(1)} %bitcast.453), kind=kOutput, calls=%fused_computation.118 | convolution fusion | flops 2217738240 | bytes 8392704 | tf_op jit(solution)/shard_map/nlcf,lfd->nlcd/dot_general | solution.py:85
  77.6 0.5 all-gather.7.cloned.1.call-start
  78.1 31.1 %reduce-scatter.5.cloned.1.call-done = bf16[8,1,32,1024]{3,2,0,1:T(8,128)(2,1)} async-done(((bf16[32,1,32,1024]{3,2,0,1:T(8,128)(2,1)}), bf16[8,1,32,1024]{3,2,0,1:T(8,128)(2,1)}) %reduce-scatter.5.cloned.1.call-update) | async-done | bytes 524304 | tf_op jit(solution)/shard_map/reduce_scatter | solution.py:92
  109.2 2.0 convert_reduce_fusion.6
  111.3 22.7 %all-gather.7.cloned.1.call-done = bf16[1024,1024]{1,0:T(8,128)(2,1)} async-done(((bf16[256,1024]{1,0:T(8,128)(2,1)}), bf16[1024,1024]{1,0:T(8,128)(2,1)}) %all-gather.7.cloned.1.call-update) | async-done | bytes 2097168 | tf_op jit(solution)/shard_map/all_gather | solution.py:69
  134.1 2.1 convert_reduce_fusion.2
  136.1 2.7 multiply_reduce_fusion
  138.8 0.8 add_convert_fusion.2
  139.7 2.3 fusion.59
  142.0 2.0 copy-done.46
  144.0 11.9 %convert_bitcast_fusion.2 = bf16[32,1,32,1024]{3,2,0,1:T(8,128)(2,1)} fusion(bf16[2,1,1024,1024]{3,2,1,0:T(8,128)(2,1)S(1)} %copy-done.36, f32[32,32,1024]{2,1,0:T(8,128)S(1)} %fusion.59, f32[1024]{0:T(1024)S(1)} %bitcast.456), kind=kOutput, calls=%fused_computation.117 | convolution fusion | flops 2217738240 | bytes 8392704 | tf_op jit(solution)/shard_map/nlcf,lfd->nlcd/dot_general | solution.py:85
  155.9 31.6 %reduce-scatter.7.cloned.1.call-done = bf16[8,1,32,1024]{3,2,0,1:T(8,128)(2,1)} async-done(((bf16[32,1,32,1024]{3,2,0,1:T(8,128)(2,1)}), bf16[8,1,32,1024]{3,2,0,1:T(8,128)(2,1)}) %reduce-scatter.7.cloned.1.call-update) | async-done | bytes 524304 | tf_op jit(solution)/shard_map/reduce_scatter | solution.py:92
  187.5 2.1 fusion.117
  189.6 5.5 %all-to-all-start.1 = ((bf16[8,32,1024]{2,1,0:T(8,128)(2,1)}), bf16[8,32,1024]{2,1,0:T(8,128)(2,1)S(1)}, u32[]{:S(2)}, u32[]{:S(2)}) async-start(bf16[8,32,1024]{2,1,0:T(8,128)(2,1)} %get-tuple-element.34), calls=%async_computation.3 | async-start | bytes 1048576 | tf_op jit(solution)/shard_map/all_to_all | solution.py:105
  195.9 0.3 fusion.109
  196.2 13.4 %all-to-all-done.1 = bf16[8,32,1024]{2,1,0:T(8,128)(2,1)S(1)} async-done(((bf16[8,32,1024]{2,1,0:T(8,128)(2,1)}), bf16[8,32,1024]{2,1,0:T(8,128)(2,1)S(1)}, u32[]{:S(2)}, u32[]{:S(2)}) %all-to-all-start.1) | async-done | bytes 524320 | tf_op jit(solution)/shard_map/all_to_all | solution.py:105
  209.6 1.2 gather_fusion.1
  210.8 0.3 fusion.122
  211.1 1.2 multiply_convert_fusion
  212.3 1.2 gather_fusion.2
  213.6 18.4 %all_to_all.43 = bf16[8,32,1024]{2,1,0:T(8,128)(2,1)} all-to-all(bf16[8,32,1024]{2,1,0:T(8,128)(2,1)S(1)} %broadcast_select_fusion), channel_id=1, replica_groups=mesh['expert'=8,'batch'=4] {'expert'}, dimensions={0} | all-to-all | bytes 1048576 | tf_op jit(solution)/shard_map/all_to_all | solution.py:115
  232.0 20.8 %all-gather.9.cloned.1.call-done = bf16[1024,1024]{1,0:T(8,128)(2,1)} async-done(((bf16[256,1024]{1,0:T(8,128)(2,1)}), bf16[1024,1024]{1,0:T(8,128)(2,1)}) %all-gather.9.cloned.1.call-update) | async-done | bytes 2097168 | tf_op jit(solution)/shard_map/all_gather | solution.py:124
  252.9 14.8 %convert_reduce_fusion = (f32[1024]{0:T(1024)}, bf16[32,1,32,1024]{3,2,0,1:T(8,128)(2,1)S(1)}) fusion(bf16[32,32,1024]{2,1,0:T(8,128)(2,1)} %bitcast.461, bf16[2,1,1024,1024]{3,2,1,0:T(8,128)(2,1)} %param.21, f32[1024]{0:T(1024)S(1)} %bitcast.457, f32[32,32,1024]{2,1,0:T(8,128)} %copy-done.46), kind=kOutput, calls=%fused_computation.45 | convolution fusion | flops 2226125824 | bytes 10493952 | tf_op jit(solution)/shard_map/nlcd,lfd->nlcf/dot_general | solution.py:128
  267.6 1.3 copy-done.42
  269.0 3.7 convert_bitcast_fusion.1
  272.9 0.3 fusion.118
  273.2 0.3 copy-done.16
  273.5 0.6 add_rsqrt_fusion
  274.4 0.2 select_reduce_fusion
  274.6 0.2 fusion.136
  274.7 40.1 %all-reduce = (f32[8,1024]{1,0:T(8,128)}, f32[8]{0:T(128)S(1)}, f32[8]{0:T(128)S(1)}) all-reduce(f32[8,1024]{1,0:T(8,128)S(1)} %fusion.136, f32[8]{0:T(128)S(1)} %get-tuple-element.20, f32[8]{0:T(128)S(1)} %get-tuple-element.19), channel_id=1, replica_groups=mesh['expert'=8,'batch'=4] {'expert','batch'}, use_global_device_ids=true, to_apply=%region_19.20 | all-reduce | flops 8208 | bytes 65664 | tf_op jit(solution)/shard_map/psum | solution.py:178
  314.9 0.5 broadcast_multiply_fusion.8
  315.4 1.1 convert_reduce_fusion.9
  316.5 6.2 %convolution_bitcast_fusion.2 = f32[1,1,1024,1024]{3,2,1,0:T(8,128)} fusion(bf16[32,1,32,1024]{3,2,0,1:T(8,128)(2,1)} %copy-done.42, f32[1024]{0:T(1024)S(1)} %bitcast.452, f32[1024]{0:T(1024)S(1)} %bitcast.438, f32[32,32]{1,0:T(8,128)S(1)} %rsqrt.45, f32[32,32]{1,0:T(8,128)S(1)} %div.70, bf16[32,32,1024]{2,1,0:T(8,128)(2,1)S(1)} %bitcast.425), kind=kOutput, calls=%fused_computation.85 | convolution fusion | flops 2153775104 | bytes 8404992 | tf_op jit(solution)/shard_map/nlcd,nlcf->ldf/dot_general | solution.py:138
  322.8 1.6 fusion.131
  324.3 2.4 convert_reduce_fusion.8
  326.7 0.3 reduce-scatter.11.cloned.1.call-start
  327.0 14.4 %convolution_bitcast_fusion = f32[1,1,1024,1024]{3,2,1,0:T(8,128)} fusion(bf16[32,32,1024]{2,1,0:T(8,128)(2,1)} %bitcast.462, f32[32,32,1024]{2,1,0:T(8,128)} %copy-done.46, f32[1024]{0:T(1024)S(1)} %bitcast.458), kind=kOutput, calls=%fused_computation.83 | convolution fusion | flops 2216689664 | bytes 10489856 | tf_op jit(solution)/shard_map/nlcf,nlcd->lfd/dot_general | solution.py:135
  341.4 8.7 %all-gather.11.cloned.1.call-done = bf16[1024,1024]{1,0:T(8,128)(2,1)} async-done(((bf16[256,1024]{1,0:T(8,128)(2,1)}), bf16[1024,1024]{1,0:T(8,128)(2,1)}) %all-gather.11.cloned.1.call-update) | async-done | bytes 2097168 | tf_op jit(solution)/shard_map/all_gather | solution.py:124
  350.1 14.4 %convert_reduce_fusion.1 = (f32[1024]{0:T(1024)S(1)}, bf16[32,1,32,1024]{3,2,0,1:T(8,128)(2,1)S(1)}) fusion(bf16[32,32,1024]{2,1,0:T(8,128)(2,1)} %bitcast.463, bf16[2,1,1024,1024]{3,2,1,0:T(8,128)(2,1)} %param.21, f32[1024]{0:T(1024)S(1)} %bitcast.454, f32[32,32,1024]{2,1,0:T(8,128)} %copy-done.44), kind=kOutput, calls=%fused_computation.46 | convolution fusion | flops 2226125824 | bytes 10493952 | tf_op jit(solution)/shard_map/nlcd,lfd->nlcf/dot_general | solution.py:128
  364.6 1.3 copy-done.43
  365.9 3.7 convert_bitcast_fusion
  369.7 6.3 %convolution_bitcast_fusion.3 = f32[1,1,1024,1024]{3,2,1,0:T(8,128)} fusion(bf16[32,1,32,1024]{3,2,0,1:T(8,128)(2,1)} %copy-done.43, f32[1024]{0:T(1024)S(1)} %bitcast.450, f32[1024]{0:T(1024)S(1)} %bitcast.434, f32[32,32]{1,0:T(8,128)S(1)} %rsqrt.44, f32[32,32]{1,0:T(8,128)S(1)} %div.69, bf16[32,32,1024]{2,1,0:T(8,128)(2,1)S(1)} %bitcast.424), kind=kOutput, calls=%fused_computation.86 | convolution fusion | flops 2153775104 | bytes 8404992 | tf_op jit(solution)/shard_map/nlcd,nlcf->ldf/dot_general | solution.py:138
  376.0 12.1 %convolution_bitcast_fusion.1 = f32[1,1,1024,1024]{3,2,1,0:T(8,128)} fusion(bf16[32,32,1024]{2,1,0:T(8,128)(2,1)S(1)} %bitcast.464, f32[32,32,1024]{2,1,0:T(8,128)S(1)} %copy-done.45, f32[1024]{0:T(1024)S(1)} %bitcast.455), kind=kOutput, calls=%fused_computation.84 | convolution fusion | flops 2216689664 | bytes 10489856 | tf_op jit(solution)/shard_map/nlcf,nlcd->lfd/dot_general | solution.py:135
  388.1 13.1 %reduce-scatter.11.cloned.1.call-done = bf16[8,1,32,1024]{3,2,0,1:T(8,128)(2,1)} async-done(((bf16[32,1,32,1024]{3,2,0,1:T(8,128)(2,1)}), bf16[8,1,32,1024]{3,2,0,1:T(8,128)(2,1)}) %reduce-scatter.11.cloned.1.call-update) | async-done | bytes 524304 | tf_op jit(solution)/shard_map/reduce_scatter | solution.py:151
  401.2 1.6 fusion.132
  402.8 2.3 fusion.134
  405.1 5.5 %all-to-all-start.3 = ((bf16[8,32,1024]{2,1,0:T(8,128)(2,1)}), bf16[8,32,1024]{2,1,0:T(8,128)(2,1)S(1)}, u32[]{:S(2)}, u32[]{:S(2)}) async-start(bf16[8,32,1024]{2,1,0:T(8,128)(2,1)} %fusion.134), calls=%async_computation.7 | async-start | bytes 1048576 | tf_op jit(solution)/shard_map/all_to_all | solution.py:174
  410.6 0.6 pad_maximum_fusion.4
  411.2 8.7 %pad_maximum_fusion.1 = f32[2,1,1024,1024]{3,2,1,0:T(8,128)} fusion(f32[1,1,1024,1024]{3,2,1,0:T(8,128)} %convolution_bitcast_fusion, f32[1,1,1024,1024]{3,2,1,0:T(8,128)} %convolution_bitcast_fusion.1), kind=kLoop, calls=%fused_computation.6 | loop fusion | flops 2097152 | bytes 16777216 | tf_op jit(solution)/shard_map/stack | solution.py:190
  419.9 4.2 pad_maximum_fusion
  424.2 11.1 %all-reduce.1 = (f32[2,1,1024]{2,1,0:T(1,128)}, f32[2,1,1024]{2,1,0:T(1,128)}, f32[2,1,1024]{2,1,0:T(1,128)}) all-reduce(f32[2,1,1024]{2,1,0:T(1,128)S(1)} %pad_maximum_fusion.2, f32[2,1,1024]{2,1,0:T(1,128)S(1)} %pad_maximum_fusion.3, f32[2,1,1024]{2,1,0:T(1,128)S(1)} %pad_maximum_fusion.5), channel_id=1, replica_groups=mesh['expert'=8,'batch'=4] {'batch'}, use_global_device_ids=true, to_apply=%region_22.23 | all-reduce | flops 6144 | bytes 49152 | tf_op jit(solution)/shard_map/psum | solution.py:171
  435.3 1.3 gather_fusion.3
  436.6 1.2 fusion.101
  (137 shorter events, 1.4 us)
Async XLA Ops:
  7.2 188.7 %copy-start = (bf16[8,1024]{1,0:T(8,128)(2,1)S(1)}, bf16[8,1024]{1,0:T(8,128)(2,1)}, u32[]{:S(2)}) copy-start(bf16[8,1024]{1,0:T(8,128)(2,1)} %param.16) | copy-start | bytes 49156
  7.2 26.9 %copy-start.23 = (bf16[2,1,1024]{2,0,1:T(2,128)(2,1)S(1)}, bf16[2,1,1024]{2,0,1:T(2,128)(2,1)}, u32[]{:S(2)}) copy-start(bf16[2,1,1024]{2,0,1:T(2,128)(2,1)} %param.17) | copy-start | bytes 12292
  7.2 26.9 %copy-start.24 = (bf16[2,1,1024]{2,0,1:T(2,128)(2,1)S(1)}, bf16[2,1,1024]{2,0,1:T(2,128)(2,1)}, u32[]{:S(2)}) copy-start(bf16[2,1,1024]{2,0,1:T(2,128)(2,1)} %param.18) | copy-start | bytes 12292
  7.2 26.9 %copy-start.25 = (bf16[2,1,1024]{2,0,1:T(2,128)(2,1)S(1)}, bf16[2,1,1024]{2,0,1:T(2,128)(2,1)}, u32[]{:S(2)}) copy-start(bf16[2,1,1024]{2,0,1:T(2,128)(2,1)} %param.20) | copy-start | bytes 12292
  7.2 48.5 %all-gather.5.cloned.1.call-start = ((), (), s32[]{:S(2)}) async-start(), calls=%async_computation.8 | async-start | bytes 2621440 | tf_op jit(solution)/shard_map/all_gather | solution.py:69
  34.0 75.2 %reduce-scatter.5.cloned.1.call-start = ((), (), s32[]{:S(2)}) async-start(), calls=%async_computation.9 | async-start | bytes 2621440 | tf_op jit(solution)/shard_map/reduce_scatter | solution.py:92
  34.1 27.3 %copy-start.19 = (f32[1,1,1024]{2,0,1:T(1,128)}, f32[1,1,1024]{2,0,1:T(1,128)S(1)}, u32[]{:S(2)}) copy-start(f32[1,1,1024]{2,0,1:T(1,128)S(1)} %get-tuple-element.40) | copy-start | bytes 12292
  34.2 27.2 %copy-start.27 = (f32[1,1,1024]{2,0,1:T(1,128)}, f32[1,1,1024]{2,0,1:T(1,128)S(1)}, u32[]{:S(2)}) copy-start(f32[1,1,1024]{2,0,1:T(1,128)S(1)} %get-tuple-element.42) | copy-start | bytes 12292
  55.8 4.8 %copy-start.4 = (bf16[1024,1024]{1,0:T(8,128)(2,1)S(1)}, bf16[1024,1024]{1,0:T(8,128)(2,1)}, u32[]{:S(2)}) copy-start(bf16[1024,1024]{1,0:T(8,128)(2,1)} %all-gather.5.cloned.1.call-done) | copy-start | bytes 6291460
  55.8 5.6 %copy-start.37 = (bf16[2,1,1024,1024]{3,2,1,0:T(8,128)(2,1)S(1)}, bf16[2,1,1024,1024]{3,2,1,0:T(8,128)(2,1)}, u32[]{:S(2)}) copy-start(bf16[2,1,1024,1024]{3,2,1,0:T(8,128)(2,1)} %param.19) | copy-start | bytes 12582916
  61.4 4.4 copy-start.35
  63.8 2.0 copy-start.44
  65.8 12.3 %copy-start.26 = (bf16[2,1,1024]{2,0,1:T(2,128)(2,1)S(1)}, bf16[2,1,1024]{2,0,1:T(2,128)(2,1)}, u32[]{:S(2)}) copy-start(bf16[2,1,1024]{2,0,1:T(2,128)(2,1)} %param.22) | copy-start | bytes 12292
  65.8 43.4 %copy-start.2 = (bf16[8,32,1024]{2,1,0:T(8,128)(2,1)S(1)}, bf16[8,32,1024]{2,1,0:T(8,128)(2,1)}, u32[]{:S(2)}) copy-start(bf16[8,32,1024]{2,1,0:T(8,128)(2,1)} %all_to_all.42) | copy-start | bytes 1572868
  77.6 56.4 %all-gather.7.cloned.1.call-start = ((), (), s32[]{:S(2)}) async-start(), calls=%async_computation.10 | async-start | bytes 2621440 | tf_op jit(solution)/shard_map/all_gather | solution.py:69
  111.3 76.2 %reduce-scatter.7.cloned.1.call-start = ((), (), s32[]{:S(2)}) async-start(), calls=%async_computation.11 | async-start | bytes 2621440 | tf_op jit(solution)/shard_map/reduce_scatter | solution.py:92
  134.0 4.8 %copy-start.6 = (bf16[1024,1024]{1,0:T(8,128)(2,1)S(1)}, bf16[1024,1024]{1,0:T(8,128)(2,1)}, u32[]{:S(2)}) copy-start(bf16[1024,1024]{1,0:T(8,128)(2,1)} %all-gather.7.cloned.1.call-done) | copy-start | bytes 6291460
  134.0 5.6 %copy-start.38 = (bf16[2,1,1024,1024]{3,2,1,0:T(8,128)(2,1)S(1)}, bf16[2,1,1024,1024]{3,2,1,0:T(8,128)(2,1)}, u32[]{:S(2)}) copy-start(bf16[2,1,1024,1024]{3,2,1,0:T(8,128)(2,1)} %param.19) | copy-start | bytes 12582916
  139.7 4.4 copy-start.36
  142.0 2.0 copy-start.46
  144.0 43.5 %copy-start.8 = (bf16[8,1,32,1024]{3,2,0,1:T(8,128)(2,1)S(1)}, bf16[8,1,32,1024]{3,2,0,1:T(8,128)(2,1)}, u32[]{:S(2)}) copy-start(bf16[8,1,32,1024]{3,2,0,1:T(8,128)(2,1)} %get-tuple-element.32) | copy-start | bytes 1572868
  155.9 40.0 %copy-start.1 = (bf16[256,1024]{1,0:T(8,128)(2,1)S(1)}, bf16[256,1024]{1,0:T(8,128)(2,1)}, u32[]{:S(2)}) copy-start(bf16[256,1024]{1,0:T(8,128)(2,1)} %param.12) | copy-start | bytes 1572868
  155.9 40.0 %copy-start.21 = (s32[256]{0:T(256)S(1)}, s32[256]{0:T(256)}, u32[]{:S(2)}) copy-start(s32[256]{0:T(256)} %param.14) | copy-start | bytes 3076
  155.9 54.9 %copy-start.14 = (bf16[256,1024]{1,0:T(8,128)(2,1)S(1)}, bf16[256,1024]{1,0:T(8,128)(2,1)}, u32[]{:S(2)}) copy-start(bf16[256,1024]{1,0:T(8,128)(2,1)} %param.23) | copy-start | bytes 1572868
  189.6 20.0 %all-to-all-start.1 = ((bf16[8,32,1024]{2,1,0:T(8,128)(2,1)}), bf16[8,32,1024]{2,1,0:T(8,128)(2,1)S(1)}, u32[]{:S(2)}, u32[]{:S(2)}) async-start(bf16[8,32,1024]{2,1,0:T(8,128)(2,1)} %get-tuple-element.34), calls=%async_computation.3 | async-start | bytes 1048576 | tf_op jit(solution)/shard_map/all_to_all | solution.py:105
  195.1 57.7 %all-gather.9.cloned.1.call-start = ((), (), s32[]{:S(2)}) async-start(), calls=%async_computation.12 | async-start | bytes 2621440 | tf_op jit(solution)/shard_map/all_gather | solution.py:124
  195.8 78.6 %copy-start.30 = (f32[256]{0:T(256)}, f32[256]{0:T(256)S(1)}, u32[]{:S(2)}) copy-start(f32[256]{0:T(256)S(1)} %compare_convert_fusion) | copy-start | bytes 3076
  195.9 16.4 %copy-start.29 = (s32[1024]{0:T(1024)}, s32[1024]{0:T(1024)S(1)}, u32[]{:S(2)}) copy-start(s32[1024]{0:T(1024)S(1)} %pad_clamp_fusion) | copy-start | bytes 12292
  211.1 63.4 %copy-start.33 = (bf16[256]{0:T(256)(128)(2,1)}, bf16[256]{0:T(256)(128)(2,1)S(1)}, u32[]{:S(2)}) copy-start(bf16[256]{0:T(256)(128)(2,1)S(1)} %get-tuple-element.29) | copy-start | bytes 1540
  232.0 90.8 %reduce-scatter.9.cloned.1.call-start = ((), (), s32[]{:S(2)}) async-start(), calls=%async_computation.13 | async-start | bytes 2621440 | tf_op jit(solution)/shard_map/reduce_scatter | solution.py:151
  252.9 16.1 %copy-start.39 = (bf16[2,1,1024,1024]{3,2,1,0:T(8,128)(2,1)S(1)}, bf16[2,1,1024,1024]{3,2,1,0:T(8,128)(2,1)}, u32[]{:S(2)}) copy-start(bf16[2,1,1024,1024]{3,2,1,0:T(8,128)(2,1)} %param.19) | copy-start | bytes 12582916
  267.6 1.3 copy-start.42
  272.7 43.8 %copy-start.7 = (bf16[1024,1024]{1,0:T(8,128)(2,1)S(1)}, bf16[1024,1024]{1,0:T(8,128)(2,1)}, u32[]{:S(2)}) copy-start(bf16[1024,1024]{1,0:T(8,128)(2,1)} %all-gather.7.cloned.1.call-done) | copy-start | bytes 6291460
  272.7 77.4 %all-gather.11.cloned.1.call-start = ((), (), s32[]{:S(2)}) async-start(), calls=%async_computation.14 | async-start | bytes 2621440 | tf_op jit(solution)/shard_map/all_gather | solution.py:124
  272.9 0.6 copy-start.16
  316.5 6.2 %copy-start.9 = (bf16[8,1,32,1024]{3,2,0,1:T(8,128)(2,1)S(1)}, bf16[8,1,32,1024]{3,2,0,1:T(8,128)(2,1)}, u32[]{:S(2)}) copy-start(bf16[8,1,32,1024]{3,2,0,1:T(8,128)(2,1)} %get-tuple-element.32) | copy-start | bytes 1572868
  316.5 7.8 %copy-start.10 = (bf16[8,32,1024]{2,1,0:T(8,128)(2,1)S(1)}, bf16[8,32,1024]{2,1,0:T(8,128)(2,1)}, u32[]{:S(2)}) copy-start(bf16[8,32,1024]{2,1,0:T(8,128)(2,1)} %all_to_all.43) | copy-start | bytes 1572868
  326.7 74.5 %reduce-scatter.11.cloned.1.call-start = ((), (), s32[]{:S(2)}) async-start(), calls=%async_computation.15 | async-start | bytes 2621440 | tf_op jit(solution)/shard_map/reduce_scatter | solution.py:151
  350.1 15.7 %copy-start.40 = (bf16[2,1,1024,1024]{3,2,1,0:T(8,128)(2,1)S(1)}, bf16[2,1,1024,1024]{3,2,1,0:T(8,128)(2,1)}, u32[]{:S(2)}) copy-start(bf16[2,1,1024,1024]{3,2,1,0:T(8,128)(2,1)} %param.19) | copy-start | bytes 12582916
  364.6 1.3 copy-start.43
  365.9 3.7 copy-start.5
  365.9 3.7 copy-start.20
  365.9 3.7 copy-start.28
  369.6 6.3 %copy-start.41 = (bf16[1024,1024]{1,0:T(8,128)(2,1)S(1)}, bf16[1024,1024]{1,0:T(8,128)(2,1)}, u32[]{:S(2)}) copy-start(bf16[1024,1024]{1,0:T(8,128)(2,1)} %all-gather.11.cloned.1.call-done) | copy-start | bytes 6291460
  369.6 6.3 %copy-start.45 = (f32[32,32,1024]{2,1,0:T(8,128)S(1)}, f32[32,32,1024]{2,1,0:T(8,128)}, u32[]{:S(2)}) copy-start(f32[32,32,1024]{2,1,0:T(8,128)} %copy-done.44) | copy-start | bytes 12582916
  376.0 25.2 %copy-start.3 = (bf16[8,32,1024]{2,1,0:T(8,128)(2,1)S(1)}, bf16[8,32,1024]{2,1,0:T(8,128)(2,1)}, u32[]{:S(2)}) copy-start(bf16[8,32,1024]{2,1,0:T(8,128)(2,1)} %all_to_all.42) | copy-start | bytes 1572868
  376.0 25.2 %copy-start.17 = (f32[8,32]{1,0:T(8,128)S(1)}, f32[8,32]{1,0:T(8,128)}, u32[]{:S(2)}) copy-start(f32[8,32]{1,0:T(8,128)} %copy-done.16) | copy-start | bytes 3076
  376.0 25.2 %copy-start.18 = (f32[8,32]{1,0:T(8,128)S(1)}, f32[8,32]{1,0:T(8,128)}, u32[]{:S(2)}) copy-start(f32[8,32]{1,0:T(8,128)} %add_rsqrt_fusion) | copy-start | bytes 3076
  376.0 26.8 %copy-start.11 = (bf16[8,1,32,1024]{3,2,0,1:T(8,128)(2,1)S(1)}, bf16[8,1,32,1024]{3,2,0,1:T(8,128)(2,1)}, u32[]{:S(2)}) copy-start(bf16[8,1,32,1024]{3,2,0,1:T(8,128)(2,1)} %get-tuple-element.28) | copy-start | bytes 1572868
  388.1 22.5 %copy-start.32 = (f32[1024]{0:T(1024)S(1)}, f32[1024]{0:T(1024)}, u32[]{:S(2)}) copy-start(f32[1024]{0:T(1024)} %get-tuple-element.47) | copy-start | bytes 12292
  405.1 30.2 %all-to-all-start.3 = ((bf16[8,32,1024]{2,1,0:T(8,128)(2,1)}), bf16[8,32,1024]{2,1,0:T(8,128)(2,1)S(1)}, u32[]{:S(2)}, u32[]{:S(2)}) async-start(bf16[8,32,1024]{2,1,0:T(8,128)(2,1)} %fusion.134), calls=%async_computation.7 | async-start | bytes 1048576 | tf_op jit(solution)/shard_map/all_to_all | solution.py:174
  411.2 8.7 %copy-start.12 = (f32[1,1,1024,1024]{3,2,1,0:T(8,128)S(1)}, f32[1,1,1024,1024]{3,2,1,0:T(8,128)}, u32[]{:S(2)}) copy-start(f32[1,1,1024,1024]{3,2,1,0:T(8,128)} %convolution_bitcast_fusion.2) | copy-start | bytes 12582916
  411.2 8.7 %copy-start.13 = (f32[1,1,1024,1024]{3,2,1,0:T(8,128)S(1)}, f32[1,1,1024,1024]{3,2,1,0:T(8,128)}, u32[]{:S(2)}) copy-start(f32[1,1,1024,1024]{3,2,1,0:T(8,128)} %convolution_bitcast_fusion.3) | copy-start | bytes 12582916
  424.1 12.4 %copy-start.15 = (bf16[256,1024]{1,0:T(8,128)(2,1)S(1)}, bf16[256,1024]{1,0:T(8,128)(2,1)}, u32[]{:S(2)}) copy-start(bf16[256,1024]{1,0:T(8,128)(2,1)} %param.23) | copy-start | bytes 1572868
  424.1 12.5 %copy-start.22 = (s32[256]{0:T(256)S(1)}, s32[256]{0:T(256)}, u32[]{:S(2)}) copy-start(s32[256]{0:T(256)} %param.14) | copy-start | bytes 3076
  424.1 12.5 %copy-start.31 = (f32[256]{0:T(256)S(1)}, f32[256]{0:T(256)}, u32[]{:S(2)}) copy-start(f32[256]{0:T(256)} %copy-done.30) | copy-start | bytes 3076
  424.1 12.5 %copy-start.34 = (bf16[256]{0:T(256)(128)(2,1)S(1)}, bf16[256]{0:T(256)(128)(2,1)}, u32[]{:S(2)}) copy-start(bf16[256]{0:T(256)(128)(2,1)} %copy-done.33) | copy-start | bytes 1540
Sparse Core Ops, SparseCore 0:
  34.1 21.5 all-gather.4
  77.7 31.4 reduce-scatter.4
  111.4 22.5 all-gather.6
  156.0 31.4 reduce-scatter.6
  232.1 20.6 all-gather.8
  272.8 31.5 reduce-scatter.8
  326.8 23.2 all-gather.10
  369.7 31.4 reduce-scatter.10
where the time goes:
time: 454 us; the launch traced here: 445 us
  waiting for transfers between devices  163 us (36%)
  matrix products  106 us (23%)
  blocking collectives  91.3 us (20%)
  other arithmetic  41.9 us (9%)
  between operations  15.9 us (4%)
  local copies, waits for them, and re-layouts  15.2 us (3%)
  starting transfers between devices  12 us (3%)
    reduce_scatter x2, waiting for transfers between devices, per_device(): lax.psum_scatter(down_part(jnp.int32(0), lax.axis_size('batch') * groups)...  62.6 us
    all_gather x2, waiting for transfers between devices, per_device(): gathered = lax.all_gather(current, 'batch', axis=0, tiled=True)  44.3 us
    psum x1, blocking collectives, per_device(): centroid_grad = lax.psum(centroid_part, ('expert', 'batch'))  40.1 us
    all_gather x2, waiting for transfers between devices, per_device(): lax.all_gather(grad_rows, 'batch', axis=0, tiled=True)  29.5 us
    dot_general x2, matrix products, per_device(): jnp.einsum('nlcd,lfd->nlcf', grads_all, down_weight[expert_layer_step], p...  29.2 us
    dot_general x2, matrix products, per_device(): jnp.einsum('nlcf,nlcd->lfd', activity, grads_all, preferred_element_type=...  26.5 us
    dot_general x2, matrix products, down_part(): jnp.einsum('nlcf,lfd->nlcd', activity, down_weight[expert_layer_step], pr...  23.7 us
    all_to_all x1, blocking collectives, per_device(): lax.all_to_all(pack(tokens), 'expert', split_axis=0, concat_axis=0, tiled...  21.7 us
  transfers between devices with their start and end apart: 10, of which 8 were waited for; matrix products, arithmetic and copies ran while one was open for 13% of the time, Pallas kernels for 0%

commit v1 on v0

--- a/solution.py
+++ b/solution.py
@@ -1,6 +1,10 @@
+import functools
+
 import jax
 import jax.numpy as jnp
 from jax import lax
+from jax.experimental import pallas as pl
+from jax.experimental.pallas import tpu as pltpu
 from jax.sharding import PartitionSpec as P
 
 
@@ -194,6 +198,688 @@
     )
 
 
+MESH = pl.DeviceIdType.MESH
+F32 = jnp.float32
+BF16 = jnp.bfloat16
+ROW_STEP = 32
+COL_STEP = 256
+EMPTY = 8.0
+LINK_KINDS = ("x", "g", "sum0", "out", "ngrad1", "ngrad0")
+CORE_KINDS = ("x", "g", "part0", "h", "part1", "ngrad1", "hgrad", "ngrad0")
+ROUTE_KINDS = ("x", "ct", "mixed", "tgrad", "totals")
+
+
+def fused_fits(mesh):
+    groups, batches = mesh.shape["expert"], mesh.shape["batch"]
+    return batches == 4 and groups == 8
+
+
+def rows_at(start, count, unit):
+    return pl.ds(pl.multiple_of(start, unit), count)
+
+
+def loop_rows(count, step, body):
+    def one(i, carry):
+        body(i * step, step)
+        return carry
+
+    lax.fori_loop(0, count // step, one, 0)
+
+
+def normalize(values):
+    centered = values - jnp.mean(values, axis=-1, keepdims=True)
+    scale = lax.rsqrt(jnp.mean(centered * centered, axis=-1, keepdims=True) + 1e-05)
+    return centered * scale, scale
+
+
+def dot(a, b, dims):
+    return lax.dot_general(a, b, (dims, ((), ())), preferred_element_type=F32)
+
+
+NN = ((1,), (0,))
+NT = ((1,), (1,))
+TN = ((0,), (0,))
+
+
+def fused_kernel(
+    groups,
+    capacity,
+    chunks,
+    ids_ref,
+    slots_ref,
+    tok_ref,
+    ct_ref,
+    cent_ref,
+    gain_ref,
+    bias_ref,
+    up_bias_ref,
+    down_bias_ref,
+    up_hbm,
+    down_hbm,
+    mixed_ref,
+    tgrad_ref,
+    totals_ref,
+    small_ref,
+    ub_ref,
+    up_grad_hbm,
+    down_grad_hbm,
+    up_w,
+    down_w,
+    perm,
+    pack_x,
+    pack_ct,
+    xa,
+    ga,
+    ha,
+    hga,
+    n_s,
+    a_s,
+    d_s,
+    part,
+    part_in,
+    half_out,
+    half_in,
+    own_out,
+    own_in,
+    ct_own,
+    gate_s,
+    lg_s,
+    back_out,
+    back_in,
+    stage,
+    acc,
+    red,
+    totals_in,
+    w_sem,
+    route_send,
+    route_recv,
+    link_send,
+    link_recv,
+    core_send,
+    core_recv,
+    red_send,
+    red_recv,
+    out_sem,
+):
+    tok_rows, width = tok_ref.shape
+    hidden = up_w.shape[2]
+    per = groups // chunks
+    rows_m = per * 4 * capacity
+    rows_h = rows_m // 2
+    rows_o = rows_m // 4
+    e = lax.axis_index("expert")
+    b = lax.axis_index("batch")
+    x = b // 2
+    c = lax.rem(b, 2)
+    sib = (e, x * 2 + (1 - c))
+    far = (e, (1 - x) * 2 + c)
+
+    def flipped(m):
+        out = jnp.int32(0)
+        bit = 1
+        while bit < groups:
+            digit = lax.rem(e // bit, 2)
+            out = out + bit * ((1 - digit) if m & bit else digit)
+            bit *= 2
+        return out
+
+    half = c * rows_h
+    sib_half = (1 - c) * rows_h
+    own = half + x * rows_o
+    pairs = [tuple(range(j * per, (j + 1) * per)) for j in range(chunks)]
+    order = [pairs[0]] + pairs[2:] + [pairs[1]]
+    place = {m: (k, i) for k, ms in enumerate(order) for i, m in enumerate(ms)}
+    order_flat = [m for ms in order for m in ms]
+
+    def at_half(k):
+        return rows_at(k * rows_m + half, rows_h, rows_h)
+
+    def at_sib_half(k):
+        return rows_at(k * rows_m + sib_half, rows_h, rows_h)
+
+    def at_own(k):
+        return rows_at(k * rows_m + own, rows_o, rows_o)
+
+    def at_all(k):
+        return pl.ds(k * rows_m, rows_m)
+
+    def copy_to(device, src, dst, send, recv):
+        return pltpu.make_async_remote_copy(
+            src_ref=src,
+            dst_ref=dst,
+            send_sem=send,
+            recv_sem=recv,
+            device_id=device,
+            device_id_type=MESH,
+        )
+
+    def route(kind, m):
+        n = ROUTE_KINDS.index(kind)
+        k, i = place[m]
+        to = flipped(m)
+        theirs = rows_at(to * capacity, capacity, capacity)
+        mine = rows_at(e * capacity, capacity, capacity)
+        if kind == "x":
+            src = pack_x.at[theirs]
+            dst = xa.at[rows_at(k * rows_m + own + i * capacity, capacity, capacity)]
+        elif kind == "ct":
+            src = pack_ct.at[theirs]
+            dst = ct_own.at[pl.ds(k * rows_o + i * capacity, capacity)]
+        elif kind == "totals":
+            src = red.at[0]
+            dst = totals_in.at[e]
+        else:
+            s = 0 if kind == "mixed" else 1
+            src = back_out.at[s, pl.ds(k * rows_o + i * capacity, capacity)]
+            dst = back_in.at[s, mine]
+        return copy_to((to, b), src, dst, route_send.at[n, m], route_recv.at[n, m])
+
+    def link(kind, k):
+        n = LINK_KINDS.index(kind)
+        if kind == "x":
+            src = dst = xa.at[at_own(k)]
+        elif kind == "g":
+            src = dst = ga.at[at_own(k)]
+        elif kind in ("sum0", "ngrad1"):
+            s = 0 if kind == "sum0" else 1
+            at = pl.ds(k * rows_h, rows_h)
+            src, dst = half_out.at[s, at], half_in.at[s, at]
+        else:
+            s = 0 if kind == "out" else 1
+            at = pl.ds(k * rows_o, rows_o)
+            src, dst = own_out.at[s, at], own_in.at[s, at]
+        return copy_to(far, src, dst, link_send.at[n, k], link_recv.at[n, k])
+
+    def core(kind, k):
+        n = CORE_KINDS.index(kind)
+        whole = {"x": xa, "g": ga, "h": ha, "hgrad": hga}
+        if kind in whole:
+            src = dst = whole[kind].at[at_half(k)]
+        else:
+            s = ("part0", "part1", "ngrad1", "ngrad0").index(kind)
+            src = part.at[s, at_sib_half(k)]
+            dst = part_in.at[s, pl.ds(k * rows_h, rows_h)]
+        return copy_to(sib, src, dst, core_send.at[n, k], core_recv.at[n, k])
+
+    barrier = pltpu.get_barrier_semaphore()
+    peers = [sib, far] + [(flipped(m), b) for m in range(1, groups)]
+    for peer in peers:
+        pl.semaphore_signal(barrier, inc=1, device_id=peer, device_id_type=MESH)
+    loads = []
+    for j in range(2):
+        loads.append(pltpu.make_async_copy(up_hbm.at[j, 0], up_w.at[j], w_sem.at[2 * j]))
+        loads.append(pltpu.make_async_copy(down_hbm.at[j, 0], down_w.at[j], w_sem.at[2 * j + 1]))
+    for load in loads:
+        load.start()
+    target = jnp.where(
+        slots_ref[...] >= 0, ids_ref[...] * capacity + slots_ref[...], -1
+    )
+    slot = lax.broadcasted_iota(jnp.int32, (tok_rows, tok_rows), 0)
+    onehot = jnp.where(slot == target, 1.0, 0.0)
+    perm[...] = onehot.astype(BF16)
+    empty = EMPTY * (1.0 - jnp.sum(onehot, axis=1, keepdims=True))
+
+    def pack(start, step):
+        cols = rows_at(start, step, step)
+        pack_x[:, cols] = (dot(perm[...], tok_ref[:, cols], NN) + empty).astype(BF16)
+        pack_ct[:, cols] = dot(perm[...], ct_ref[:, cols], NN).astype(BF16)
+
+    loop_rows(width, COL_STEP, pack)
+    acc[...] = jnp.zeros_like(acc)
+    cent_rows = cent_ref[...].astype(F32)
+    cent_at = lax.broadcasted_iota(jnp.int32, cent_rows.shape, 0)
+    cent = jnp.sum(jnp.where(cent_at == e, cent_rows, 0.0), axis=0, keepdims=True)
+    pl.semaphore_wait(barrier, len(peers))
+    for kind in ("x", "ct"):
+        for m in order_flat[1:]:
+            route(kind, m).start()
+    mine = rows_at(e * capacity, capacity, capacity)
+    xa[rows_at(own, capacity, capacity)] = pack_x[mine]
+    ct_own[pl.ds(0, capacity)] = pack_ct[mine]
+
+    def send_x(k):
+        for m in order[k]:
+            if m:
+                route("x", m).wait_recv()
+        link("x", k).start()
+
+    def send_g(k):
+        for m in order[k]:
+            if m:
+                route("ct", m).wait_recv()
+
+        def gated(start, step):
+            at = rows_at(k * rows_m + own + start, step, step)
+            at_o = rows_at(k * rows_o + start, step, step)
+            values = xa[at].astype(F32)
+            logit = jnp.sum(values * cent, axis=-1, keepdims=True)
+            gate = jax.nn.sigmoid(logit)
+            gate_s[at_o] = jnp.broadcast_to(gate, (step, 128))
+            ga[at] = (gate * ct_own[at_o].astype(F32)).astype(BF16)
+            used = jnp.where(values[:, 0:1] < 7.0, 1.0, 0.0)
+            acc[5:6] += jnp.broadcast_to(
+                jnp.sum(used * gate, axis=0, keepdims=True), (1, width)
+            )
+            acc[6:7] += jnp.broadcast_to(jnp.sum(used, axis=0, keepdims=True), (1, width))
+
+        loop_rows(rows_o, ROW_STEP, gated)
+        link("g", k).start()
+
+    def spread(kind, k):
+        link(kind, k).wait_recv()
+        core(kind, k).start()
+
+    def up_step(j, rows_ref, k):
+        gain = gain_ref[j].astype(F32)
+        bias = bias_ref[j].astype(F32)
+
+        def norm(start, step):
+            at = rows_at(k * rows_m + start, step, step)
+            rhat, _ = normalize(rows_ref[at].astype(F32))
+            n_s[j, at] = (rhat * gain + bias).astype(BF16)
+
+        loop_rows(rows_m, ROW_STEP, norm)
+
+        def up(start, step):
+            cols = rows_at(start, step, step)
+            pre = dot(n_s[j, at_all(k)], up_w[j, :, cols], NN) + up_bias_ref[j, :, cols].astype(
+                F32
+            )
+            cdf = 0.5 * (1.0 + lax.erf(pre * (0.5**0.5)))
+            pdf = jnp.exp(-0.5 * pre * pre) * 0.3989422804014327
+            a_s[j, at_all(k), cols] = (pre * cdf).astype(BF16)
+            d_s[j, at_all(k), cols] = (cdf + pre * pdf).astype(BF16)
+
+        loop_rows(hidden, COL_STEP, up)
+
+    def down_step(j, k):
+        kind = "part%d" % j
+
+        def down(start, step):
+            cols = rows_at(start, step, step)
+            part[j, at_all(k), cols] = dot(a_s[j, at_all(k)], down_w[j, :, cols], NN).astype(BF16)
+
+        loop_rows(width, COL_STEP, down)
+        core(kind, k).start()
+
+    def back_step(j, grads_ref, k):
+        kind = "ngrad%d" % j
+        s = 3 - j
+
+        def act(start, step):
+            cols = rows_at(start, step, step)
+            grad = dot(grads_ref[at_all(k)], down_w[j, cols, :], NT)
+            d_s[j, at_all(k), cols] = (grad * d_s[j, at_all(k), cols].astype(F32)).astype(BF16)
+
+        loop_rows(hidden, COL_STEP, act)
+
+        def up(start, step):
+            cols = rows_at(start, step, step)
+            part[s, at_all(k), cols] = dot(d_s[j, at_all(k)], up_w[j, cols, :], NT).astype(BF16)
+
+        loop_rows(width, COL_STEP, up)
+        core(kind, k).start()
+
+    def sum_half(kind, link_kind, k):
+        s = ("part0", "part1", "ngrad1", "ngrad0").index(kind)
+        o = ("sum0", "ngrad1").index(link_kind)
+        core(kind, k).wait_recv()
+
+        def add(start, step):
+            at = rows_at(k * rows_m + half + start, step, step)
+            at_h = rows_at(k * rows_h + start, step, step)
+            total = part[s, at].astype(F32) + part_in[s, at_h].astype(F32)
+            half_out[o, at_h] = total.astype(BF16)
+
+        loop_rows(rows_h, ROW_STEP, add)
+        link(link_kind, k).start()
+
+    def sum_far(kind, link_kind, k):
+        s = ("part0", "part1", "ngrad1", "ngrad0").index(kind)
+        o = ("out", "ngrad0").index(link_kind)
+        core(kind, k).wait_recv()
+
+        def add(start, step):
+            at = rows_at(k * rows_m + half + (1 - x) * rows_o + start, step, step)
+            at_h = rows_at(k * rows_h + (1 - x) * rows_o + start, step, step)
+            at_o = rows_at(k * rows_o + start, step, step)
+            total = part[s, at].astype(F32) + part_in[s, at_h].astype(F32)
+            own_out[o, at_o] = total.astype(BF16)
+
+        loop_rows(rows_o, ROW_STEP, add)
+        link(link_kind, k).start()
+
+    def sum_own(s, o, k, start, step):
+        at = rows_at(k * rows_m + own + start, step, step)
+        at_h = rows_at(k * rows_h + x * rows_o + start, step, step)
+        at_o = rows_at(k * rows_o + start, step, step)
+        mine = part[s, at].astype(F32) + part_in[s, at_h].astype(F32)
+        return mine + own_in[o, at_o].astype(F32)
+
+    def make_h(k):
+        link("sum0", k).wait_recv()
+        shift = down_bias_ref[0].astype(F32)
+
+        def add(start, step):
+            at = rows_at(k * rows_m + half + start, step, step)
+            at_h = rows_at(k * rows_h + start, step, step)
+            total = half_out[0, at_h].astype(F32) + half_in[0, at_h].astype(F32)
+            ha[at] = (xa[at].astype(F32) + total + shift).astype(BF16)
+
+        loop_rows(rows_h, ROW_STEP, add)
+        core("h", k).start()
+
+    def norm_back(rows, ngrad, gain):
+        rhat, scale = normalize(rows)
+        q = ngrad * gain
+        back = scale * (
+            q - jnp.mean(q, axis=-1, keepdims=True) - rhat * jnp.mean(q * rhat, axis=-1, keepdims=True)
+        )
+        return back, rhat
+
+    def make_hgrad(k):
+        link("ngrad1", k).wait_recv()
+        gain = gain_ref[1].astype(F32)
+
+        def grad(start, step):
+            at = rows_at(k * rows_m + half + start, step, step)
+            at_h = rows_at(k * rows_h + start, step, step)
+            ngrad = half_out[1, at_h].astype(F32) + half_in[1, at_h].astype(F32)
+            back, rhat = norm_back(ha[at].astype(F32), ngrad, gain)
+            hga[at] = (ga[at].astype(F32) + back).astype(BF16)
+            acc[1:2] += 0.5 * jnp.sum(ngrad * rhat, axis=0, keepdims=True)
+            acc[3:4] += 0.5 * jnp.sum(ngrad, axis=0, keepdims=True)
+
+        loop_rows(rows_h, ROW_STEP, grad)
+        core("hgrad", k).start()
+
+    def give_back(kind, k):
+        for m in order[k]:
+            if m:
+                route(kind, m).start()
+            else:
+                s = 0 if kind == "mixed" else 1
+                _, i = place[0]
+                back_in[s, mine] = back_out[s, pl.ds(k * rows_o + i * capacity, capacity)]
+
+    def make_mixed(k):
+        link("out", k).wait_recv()
+        shift = down_bias_ref[1].astype(F32)
+
+        def mix(start, step):
+            at = rows_at(k * rows_m + own + start, step, step)
+            at_o = rows_at(k * rows_o + start, step, step)
+            out = (ha[at].astype(F32) + sum_own(1, 0, k, start, step) + shift).astype(BF16).astype(F32)
+            rows = xa[at].astype(F32)
+            gate = gate_s[at_o][:, 0:1]
+            back_out[0, at_o] = (rows + gate * out).astype(BF16)
+            along = jnp.sum(ct_own[at_o].astype(F32) * out, axis=-1, keepdims=True)
+            lgrad = (along * gate * (1.0 - gate)).astype(BF16).astype(F32)
+            lg_s[at_o] = jnp.broadcast_to(lgrad, (step, 128))
+            acc[4:5] += jnp.sum(lgrad * rows, axis=0, keepdims=True)
+
+        loop_rows(rows_o, ROW_STEP, mix)
+        give_back("mixed", k)
+
+    def make_tgrad(k):
+        link("ngrad0", k).wait_recv()
+        gain = gain_ref[0].astype(F32)
+
+        def grad(start, step):
+            at = rows_at(k * rows_m + own + start, step, step)
+            at_o = rows_at(k * rows_o + start, step, step)
+            ngrad = sum_own(3, 1, k, start, step)
+            back, rhat = norm_back(xa[at].astype(F32), ngrad, gain)
+            back = (hga[at].astype(F32) + back).astype(BF16).astype(F32)
+            back_out[1, at_o] = (
+                ct_own[at_o].astype(F32) + lg_s[at_o][:, 0:1] * cent + back
+            ).astype(BF16)
+            acc[0:1] += jnp.sum(ngrad * rhat, axis=0, keepdims=True)
+            acc[2:3] += jnp.sum(ngrad, axis=0, keepdims=True)
+
+        loop_rows(rows_o, ROW_STEP, grad)
+        give_back("tgrad", k)
+
+    def column_sums(rows_ref):
+        def one(i, total):
+            values = rows_ref[rows_at(i * ROW_STEP, ROW_STEP, ROW_STEP)].astype(F32)
+            return total + jnp.sum(values, axis=0, keepdims=True)
+
+        return lax.fori_loop(
+            0, rows_ref.shape[0] // ROW_STEP, one, jnp.zeros((1, rows_ref.shape[1]), F32)
+        )
+
+    def weight_grads(j, grads_ref):
+        small_ref[4 + j : 5 + j] = column_sums(grads_ref)
+        ub_ref[j : j + 1] = column_sums(d_s.at[j])
+        for into, left, right in (
+            (down_grad_hbm, a_s.at[j], grads_ref),
+            (up_grad_hbm, n_s.at[j], d_s.at[j]),
+        ):
+            tiles = left.shape[1] // COL_STEP
+
+            def tile_copy(t):
+                at = rows_at(t * COL_STEP, COL_STEP, COL_STEP)
+                slot = lax.rem(t, 2)
+                return pltpu.make_async_copy(stage.at[slot], into.at[j, 0, at], out_sem.at[slot])
+
+            def one(t, carry):
+                @pl.when(t >= 2)
+                def _():
+                    tile_copy(t - 2).wait()
+
+                at = rows_at(t * COL_STEP, COL_STEP, COL_STEP)
+                stage[lax.rem(t, 2)] = dot(left[:, at], right[...], TN).astype(BF16)
+                tile_copy(t).start()
+                return carry
+
+            lax.fori_loop(0, tiles, one, 0)
+            tile_copy(tiles - 2).wait()
+            tile_copy(tiles - 1).wait()
+
+    steps = range(chunks)
+    for k in steps:
+        send_x(k)
+    spread("x", 0)
+    send_g(0)
+    for j in range(2):
+        loads[j].wait()
+    for k in steps:
+        core("x", k).wait_recv()
+        up_step(0, xa, k)
+        if k + 1 < chunks:
+            spread("x", k + 1)
+            send_g(k + 1)
+        if k > 0:
+            sum_half("part0", "sum0", k - 1)
+        down_step(0, k)
+        if k > 1:
+            make_h(k - 2)
+        spread("g", k)
+    sum_half("part0", "sum0", chunks - 1)
+    make_h(chunks - 2)
+    for j in range(2, 4):
+        loads[j].wait()
+    for k in steps:
+        core("h", k).wait_recv()
+        up_step(1, ha, k)
+        if k == 0:
+            make_h(chunks - 1)
+        core("g", k).wait_recv()
+        back_step(1, ga, k)
+        down_step(1, k)
+        sum_half("ngrad1", "ngrad1", k)
+        sum_far("part1", "out", k)
+        if k > 1:
+            make_hgrad(k - 2)
+            make_mixed(k - 2)
+    weight_grads(1, ga)
+    for k in steps:
+        if k >= chunks - 2:
+            make_hgrad(k)
+            make_mixed(k)
+        core("hgrad", k).wait_recv()
+        back_step(0, hga, k)
+        sum_far("ngrad0", "ngrad0", k)
+        if k > 0:
+            make_tgrad(k - 1)
+    weight_grads(0, hga)
+    make_tgrad(chunks - 1)
+
+    red[1] = acc[...]
+    over = copy_to(sib, red.at[1], red.at[2], red_send.at[0], red_recv.at[0])
+    over.start()
+    over.wait_recv()
+    red[3] = red[1] + red[2]
+    across = copy_to(far, red.at[3], red.at[4], red_send.at[1], red_recv.at[1])
+    across.start()
+    across.wait_recv()
+    red[0] = red[3] + red[4]
+    totals_in[e] = red[0]
+    for m in order_flat[1:]:
+        route("totals", m).start()
+    small_ref[0:4] = red[0, 0:4]
+
+    def unpack(kind, out_ref):
+        s = 0 if kind == "mixed" else 1
+        for m in order_flat[1:]:
+            route(kind, m).wait_recv()
+
+        def one(start, step):
+            cols = rows_at(start, step, step)
+            out_ref[:, cols] = dot(perm[...], back_in[s, :, cols], TN).astype(BF16)
+
+        loop_rows(width, COL_STEP, one)
+
+    unpack("mixed", mixed_ref)
+    unpack("tgrad", tgrad_ref)
+    for m in order_flat[1:]:
+        route("totals", m).wait_recv()
+    totals_ref[...] = totals_in[...]
+    over.wait_send()
+    across.wait_send()
+    for m in order_flat[1:]:
+        for kind in ROUTE_KINDS:
+            route(kind, m).wait_send()
+    for k in steps:
+        for kind in LINK_KINDS:
+            link(kind, k).wait_send()
+        for kind in CORE_KINDS:
+            core(kind, k).wait_send()
+
+
+def per_device_fused(
+    tokens,
+    lengths,
+    expert_ids,
+    slots,
+    centroids,
+    sublayer_norm_gain,
+    sublayer_norm_bias,
+    up_weight,
+    up_bias,
+    down_weight,
+    down_bias,
+    cotangent,
+):
+    tok_rows, width = tokens.shape
+    groups = lax.axis_size("expert")
+    batches = lax.axis_size("batch")
+    experts = centroids.shape[0]
+    capacity = tok_rows // experts
+    hidden = up_weight.shape[3]
+    chunks = 4
+    total = groups * batches * capacity
+    vmem = pl.BlockSpec(memory_space=pltpu.VMEM)
+    hbm = pl.BlockSpec(memory_space=pl.ANY)
+    outs = pl.pallas_call(
+        functools.partial(fused_kernel, groups, capacity, chunks),
+        out_shape=[
+            jax.ShapeDtypeStruct((tok_rows, width), BF16),
+            jax.ShapeDtypeStruct((tok_rows, width), BF16),
+            jax.ShapeDtypeStruct((groups, 8, width), F32),
+            jax.ShapeDtypeStruct((8, width), F32),
+            jax.ShapeDtypeStruct((8, hidden), F32),
+            jax.ShapeDtypeStruct(up_weight.shape, BF16),
+            jax.ShapeDtypeStruct(down_weight.shape, BF16),
+        ],
+        in_specs=[vmem] * 9 + [hbm] * 2,
+        out_specs=[vmem] * 5 + [hbm] * 2,
+        scratch_shapes=[
+            pltpu.VMEM((2, width, hidden), BF16),
+            pltpu.VMEM((2, hidden, width), BF16),
+            pltpu.VMEM((tok_rows, tok_rows), BF16),
+            pltpu.VMEM((tok_rows, width), BF16),
+            pltpu.VMEM((tok_rows, width), BF16),
+            pltpu.VMEM((total, width), BF16),
+            pltpu.VMEM((total, width), BF16),
+            pltpu.VMEM((total, width), BF16),
+            pltpu.VMEM((total, width), BF16),
+            pltpu.VMEM((2, total, width), BF16),
+            pltpu.VMEM((2, total, hidden), BF16),
+            pltpu.VMEM((2, total, hidden), BF16),
+            pltpu.VMEM((4, total, width), BF16),
+            pltpu.VMEM((4, total // 2, width), BF16),
+            pltpu.VMEM((2, total // 2, width), BF16),
+            pltpu.VMEM((2, total // 2, width), BF16),
+            pltpu.VMEM((2, total // 4, width), BF16),
+            pltpu.VMEM((2, total // 4, width), BF16),
+            pltpu.VMEM((tok_rows, width), BF16),
+            pltpu.VMEM((tok_rows, 128), F32),
+            pltpu.VMEM((tok_rows, 128), F32),
+            pltpu.VMEM((2, tok_rows, width), BF16),
+            pltpu.VMEM((2, tok_rows, width), BF16),
+            pltpu.VMEM((2, COL_STEP, width), BF16),
+            pltpu.VMEM((8, width), F32),
+            pltpu.VMEM((5, 8, width), F32),
+            pltpu.VMEM((groups, 8, width), F32),
+            pltpu.SemaphoreType.DMA((4,)),
+            pltpu.SemaphoreType.DMA((len(ROUTE_KINDS), groups)),
+            pltpu.SemaphoreType.DMA((len(ROUTE_KINDS), groups)),
+            pltpu.SemaphoreType.DMA((len(LINK_KINDS), chunks)),
+            pltpu.SemaphoreType.DMA((len(LINK_KINDS), chunks)),
+            pltpu.SemaphoreType.DMA((len(CORE_KINDS), chunks)),
+            pltpu.SemaphoreType.DMA((len(CORE_KINDS), chunks)),
+            pltpu.SemaphoreType.DMA((2,)),
+            pltpu.SemaphoreType.DMA((2,)),
+            pltpu.SemaphoreType.DMA((2,)),
+        ],
+        compiler_params=pltpu.CompilerParams(
+            collective_id=0, has_side_effects=True, vmem_limit_bytes=62 << 20
+        ),
+        cost_estimate=pl.CostEstimate(
+            flops=24 * total * width * hidden, bytes_accessed=40 << 20, transcendentals=0
+        ),
+    )(
+        expert_ids.reshape(1, tok_rows),
+        slots.reshape(1, tok_rows),
+        tokens,
+        cotangent,
+        centroids,
+        sublayer_norm_gain,
+        sublayer_norm_bias,
+        up_bias,
+        down_bias,
+        up_weight,
+        down_weight,
+    )
+    mixed, tokens_grad, totals, small, ub, up_grad, down_grad = outs
+    denominator = jnp.float32(capacity * groups * batches)
+    return (
+        mixed,
+        tokens_grad,
+        totals[:, 4],
+        small[0:2][:, None],
+        small[2:4][:, None],
+        up_grad.astype(F32),
+        ub[0:2][:, None],
+        down_grad.astype(F32),
+        small[4:6][:, None],
+        totals[:, 5, 0] / denominator,
+        totals[:, 6, 0] / denominator,
+    )
+
+
 def solution(mesh):
     in_specs = (
         P(("expert", "batch"), None),
@@ -222,6 +908,7 @@
         P(),
         P(),
     )
+    body = per_device_fused if fused_fits(mesh) else per_device
     return jax.shard_map(
-        per_device, mesh=mesh, in_specs=in_specs, out_specs=out_specs, check_vma=False
+        body, mesh=mesh, in_specs=in_specs, out_specs=out_specs, check_vma=False
     )

time: 454 us -> 182 us (0.40); the launches traced: 445 us -> 181 us
  waiting for transfers between devices: 163 us -> 0 us
  Pallas kernels: 0 us -> 156 us
  matrix products: 106 us -> 0 us
  blocking collectives: 91.3 us -> 0 us
  other arithmetic: 41.9 us -> 12.7 us
  between operations: 15.9 us -> 0.67 us
  starting transfers between devices: 12 us -> 0 us
    pallas_call x0 -> x1, Pallas kernels: none -> 156 us  [per_device_fused(): pl.pallas_call(functools.partial(fused_kernel, groups, capacity, chunks),...]
    dot_general x15 -> x0, matrix products: 106 us -> none  [the longest x2 29.2 us: per_device(): jnp.einsum('nlcd,lfd->nlcf', grads_all, down_weight[expert_layer_step], p...]
    reduce_scatter x4 -> x0, waiting for transfers between devices: 75.7 us -> none  [the longest x2 62.6 us: per_device(): lax.psum_scatter(down_part(jnp.int32(0), lax.axis_size('batch') * groups)...]
    all_gather x4 -> x0, waiting for transfers between devices: 73.9 us -> none  [the longest x2 44.3 us: per_device(): gathered = lax.all_gather(current, 'batch', axis=0, tiled=True)]
    psum x2 -> x0, blocking collectives: 51.2 us -> none  [the longest x1 40.1 us: per_device(): centroid_grad = lax.psum(centroid_part, ('expert', 'batch'))]
    all_to_all x2 -> x0, blocking collectives: 40.1 us -> none  [the longest x1 21.7 us: per_device(): lax.all_to_all(pack(tokens), 'expert', split_axis=0, concat_axis=0, tiled...]
    reduce_sum x14 -> x0, other arithmetic: 21.1 us -> none  [the longest x4 7.69 us: apply_layer_norm(): jnp.mean(centered * centered, axis=-1, keepdims=True) + 1e-05]
    another operation x6 -> x0, other arithmetic: 13.5 us -> none  [the longest x1 8.66 us: per_device(): jnp.stack(down_weight_grads)]
  transfers between devices with their start and end apart: 10 -> 0, of which waited for: 8 -> 0; matrix products, arithmetic and copies ran while one was open for 13% -> 0% of each run, Pallas kernels for 0% -> 0%
where the time goes in v1:
time: 182 us; the launch traced here: 181 us
  Pallas kernels  156 us (86%)
  other arithmetic  12.7 us (7%)
  local copies, waits for them, and re-layouts  11.7 us (6%)
    pallas_call x1, Pallas kernels, per_device_fused(): pl.pallas_call(functools.partial(fused_kernel, groups, capacity, chunks),...  156 us
    unnamed x17, local copies, waits for them, and re-layouts  9.81 us
    convert_element_type x1, other arithmetic, per_device_fused(): up_grad.astype(F32)  6.79 us
    convert_element_type x1, other arithmetic, per_device_fused(): down_grad.astype(F32)  4.43 us

profile of v1, /device:TPU:0, one launch (start us, length us, event | category | flops | bytes accessed | tf_op | source)
XLA Modules:
  0.0 181.5 jit_solution(2542799543282190935)
XLA Ops:
  0.6 1.3 copy.30.gain_ref
  1.9 1.3 copy.31.bias_ref
  3.2 1.3 copy.32.up_bias_ref
  4.5 1.3 copy.33.down_bias_ref
  5.8 156.4 %shard_map.194 = (bf16[256,1024]{1,0:T(8,128)(2,1)}, bf16[256,1024]{1,0:T(8,128)(2,1)}, f32[8,8,1024]{2,1,0:T(8,128)}, f32[8,1024]{1,0:T(8,128)}, f32[8,1024]{1,...) custom-call(s32[1,256]{1,0:T(1,128)} %bitcast.14, s32[1,256]{1,0:T(1,128)} %bitcast.15, ...), custom_call_target="tpu_custom_call" | custom-call | flops 25769803776 | bytes 41943040 | tf_op jit(solution)/shard_map/pallas_call | solution.py:795
  162.2 1.5 multiply_reduce_fusion
  163.7 1.0 slice.21
  164.7 0.6 copy.40
  165.3 0.9 slice_bitcast_fusion
  166.2 0.6 copy.37
  166.8 0.6 copy.35
  167.4 0.6 copy.34
  168.0 0.6 copy.36
  168.6 0.0 copy-start
  168.6 6.8 %convert_element_type.6 = f32[2,1,1024,1024]{3,2,1,0:T(8,128)} convert(bf16[2,1,1024,1024]{3,2,1,0:T(8,128)(2,1)} %get-tuple-element.22) | non-fusion elementwise | flops 2097152 | bytes 12582912 | tf_op jit(solution)/shard_map/convert_element_type | solution.py:874
  175.4 0.0 copy-done
  175.4 0.0 copy-start.2
  175.4 0.0 copy-start.1
  175.4 4.4 %convert_element_type.7 = f32[2,1,1024,1024]{3,2,1,0:T(8,128)} convert(bf16[2,1,1024,1024]{3,2,1,0:T(8,128)(2,1)S(1)} %copy-done) | non-fusion elementwise | flops 2097152 | bytes 12582912 | tf_op jit(solution)/shard_map/convert_element_type | solution.py:876
  179.9 0.0 copy-done.2
  179.9 0.8 copy.43
  180.7 0.0 copy-done.1
  180.7 0.8 copy.44
Async XLA Ops:
  168.6 6.8 %copy-start = (bf16[2,1,1024,1024]{3,2,1,0:T(8,128)(2,1)S(1)}, bf16[2,1,1024,1024]{3,2,1,0:T(8,128)(2,1)}, u32[]{:S(2)}) copy-start(bf16[2,1,1024,1024]{3,2,1,0:T(8,128)(2,1)} %get-tuple-element.24) | copy-start | bytes 12582916
  175.4 4.4 %copy-start.2 = (bf16[256,1024]{1,0:T(8,128)(2,1)S(1)}, bf16[256,1024]{1,0:T(8,128)(2,1)}, u32[]{:S(2)}) copy-start(bf16[256,1024]{1,0:T(8,128)(2,1)} %get-tuple-element.64) | copy-start | bytes 1572868
  175.4 5.2 %copy-start.1 = (bf16[256,1024]{1,0:T(8,128)(2,1)S(1)}, bf16[256,1024]{1,0:T(8,128)(2,1)}, u32[]{:S(2)}) copy-start(bf16[256,1024]{1,0:T(8,128)(2,1)} %get-tuple-element.65) | copy-start | bytes 1572868
